TPU v7x, 768 devices: a whole 4x8x12 slice. The times are simulated.
768 devices in a mesh: rep: 12 (over z), fsdp: 32 (over x, y), sub: 2 (over core).
Axes of the slice: x: 4, y: 8, z: 12, core: 2. Of those that a mesh axis runs over, the one named last changes fastest.
Arguments:
- grads: bfloat16 [12, 64, 3584, 288], P('rep', None, ('fsdp', 'sub')), may hold values from -6 to 6
- momentum: bfloat16 [64, 3584, 288], P(None, ('fsdp', 'sub')), may hold values from -18 to 18
- owner: int32 [64], replicated, may hold values from 0 to 63, each once
Outputs:
- new_momentum: bfloat16 [64, 3584, 288], P(None, ('fsdp', 'sub'))
- update: bfloat16 [64, 3584, 288], P(None, ('fsdp', 'sub'))
- owned_update: bfloat16 [64, 3584, 288], P(('fsdp', 'sub'))
Inputs may be any that keep to these rules, and one draw needn't show every extreme that they name: owner is a permutation: each group device owns exactly one matrix.
All inputs are finite; a program needn't handle non-finite values.
Results may differ from a plain program's by a relative error of at most 0.034.
Values may be sent and summed in bfloat16 or wider, within the bound.
No kernel may reach another device: no remote copies, remote signals or barrier semaphores. Data moves between devices by JAX's collectives and lax.ppermute only.
A program may use at most 64 MiB of HBM per device.

v0:
```python
import jax
import jax.numpy as jnp
from jax import lax
from jax.sharding import PartitionSpec as P

ITERS = 3


def orthogonal(ahead, width):
    whole = ahead.astype(jnp.float32)
    scale = jnp.sqrt(jnp.sum(whole * whole)) + 1e-07
    ycur = (whole / scale).astype(jnp.bfloat16)
    for step in range(ITERS):
        gram = lax.dot_general(
            ycur, ycur, (((0,), (0,)), ((), ())), preferred_element_type=jnp.float32
        ).astype(jnp.bfloat16)
        square = jnp.dot(gram, gram, preferred_element_type=jnp.float32)
        mixed = (-4.775 * gram.astype(jnp.float32) + 2.0315 * square).astype(jnp.bfloat16)
        ycur = (
            3.4445 * ycur.astype(jnp.float32)
            + jnp.dot(ycur, mixed, preferred_element_type=jnp.float32)
        ).astype(jnp.bfloat16)
    factor = 0.2 * max(ahead.shape[0], width) ** 0.5
    return (factor * ycur.astype(jnp.float32)).astype(jnp.bfloat16)


def body(grads, momentum, owner):
    width = grads.shape[3]
    total = lax.psum(grads[0], "rep").astype(jnp.float32)
    moment = 0.95 * momentum.astype(jnp.float32) + total
    new_momentum = moment.astype(jnp.bfloat16)
    ahead = (total + 0.95 * moment).astype(jnp.bfloat16)
    inverse = jnp.argsort(owner)
    outgoing = jnp.take(ahead, inverse, axis=0)
    count, rows, cols = outgoing.shape
    arrived = lax.all_to_all(outgoing, ("fsdp", "sub"), split_axis=0, concat_axis=1, tiled=True)
    owned_rows = arrived.reshape(count * rows, cols)
    result = orthogonal(owned_rows, width)
    pieces = result.reshape(count, rows, width)
    returned = lax.all_to_all(pieces, ("fsdp", "sub"), split_axis=0, concat_axis=0, tiled=True)
    update = jnp.take(returned, owner, axis=0)
    return (new_momentum, update, result[None])


def solution(mesh):
    placed = (P("rep", None, ("fsdp", "sub"), None), P(None, ("fsdp", "sub"), None), P())
    return jax.shard_map(
        body,
        mesh=mesh,
        in_specs=placed,
        out_specs=(
            P(None, ("fsdp", "sub"), None),
            P(None, ("fsdp", "sub"), None),
            P(("fsdp", "sub"), None, None),
        ),
        check_vma=False,
    )
```

profile of v0, /device:TPU:1, one launch (start us, length us, event | category | flops | bytes accessed | tf_op | source)
XLA Modules:
  0.0 342.8 jit_solution(9600384600085087911)
XLA Ops:
  7.2 0.0 all-reduce.2.cloned.1.call-start
  7.2 0.7 all-reduce.2.cloned.1.call-update
  7.9 2.0 sort.17
  10.0 126.3 %all-reduce.2.cloned.1.call-done = bf16[64,56,288]{2,1,0:T(8,128)(2,1)} async-done(((bf16[64,56,288]{2,1,0:T(8,128)(2,1)}), bf16[64,56,288]{2,1,0:T(8,128)(2,1)}) %all-reduce.2.cloned.1.call-update) | async-done | bytes 2064400 | tf_op jit(solution)/shard_map/psum | solution.py:29
  136.3 5.5 %fusion = (bf16[64,56,288]{2,1,0:T(8,128)(2,1)S(1)}, bf16[64,56,288]{2,1,0:T(8,128)(2,1)}) fusion(bf16[64,56,288]{2,1,0:T(8,128)(2,1)} %all-reduce.2.cloned.1.call-done, bf16[64,56,288]{2,1,0:T(8,128)(2,1)} %param.6), kind=kLoop, calls=%fused_computation.9 | loop fusion | flops 8257536 | bytes 8257536 | tf_op jit(solution)/shard_map/convert_element_type | solution.py:32
  141.8 2.5 gather_fusion
  144.3 2.2 broadcast_select_fusion.1
  146.4 81.9 %all_to_all.14 = bf16[64,56,288]{2,1,0:T(8,128)(2,1)S(1)} all-to-all(bf16[64,56,288]{2,1,0:T(8,128)(2,1)S(1)} %broadcast_select_fusion.1), channel_id=1, replica_groups=mesh['rep'=12,'fsdp'=32,'sub'=2] {'fsdp','sub'}, dimensions={0} | all-to-all | bytes 4128768 | tf_op jit(solution)/shard_map/all_to_all | solution.py:36
  228.3 2.0 fusion.1
  231.0 0.7 fusion.2
  231.7 1.3 fusion.16
  233.0 1.6 copy.11
  234.6 2.5 copy.12
  237.2 4.5 %fusion.4 = bf16[3584,288]{0,1:T(8,128)(2,1)} fusion(bf16[3584,288]{1,0:T(8,128)(2,1)S(1)} %bitcast.25, bf16[3584,288]{0,1:T(8,128)(2,1)} %copy.12, bf16[288,288]{1,0:T(8,128)(2,1)S(1)} %fusion.16), kind=kOutput, calls=%fused_computation.13 | convolution fusion | flops 646861824 | bytes 6359040 | tf_op jit(solution)/shard_map/dot_general | solution.py:21
  241.6 3.6 %convolution_convert_fusion.1 = bf16[288,288]{1,0:T(8,128)(2,1)S(1)} fusion(bf16[3584,288]{0,1:T(8,128)(2,1)} %fusion.4), kind=kOutput, calls=%fused_computation.33 | convolution fusion | flops 594625536 | bytes 2230272 | tf_op jit(solution)/shard_map/dot_general | solution.py:14
  245.2 2.9 fusion.5
  248.1 3.4 %convolution_convert_fusion = bf16[288,288]{1,0:T(8,128)(2,1)S(1)} fusion(bf16[3584,288]{0,1:T(8,128)(2,1)} %fusion.5), kind=kOutput, calls=%fused_computation.32 | convolution fusion | flops 594625536 | bytes 2230272 | tf_op jit(solution)/shard_map/dot_general | solution.py:14
  251.6 3.9 %fusion.9 = bf16[3584,288]{0,1:T(8,128)(2,1)S(1)} fusion(bf16[3584,288]{0,1:T(8,128)(2,1)} %fusion.5, bf16[288,288]{1,0:T(8,128)(2,1)S(1)} %convolution_convert_fusion), kind=kOutput, calls=%fused_computation.18 | convolution fusion | flops 649958400 | bytes 4294656 | tf_op jit(solution)/shard_map/dot_general | solution.py:21
  255.5 0.0 copy-start
  255.5 3.0 copy.13
  258.4 6.3 %all-to-all-start.1 = ((bf16[64,56,288]{2,1,0:T(8,128)(2,1)}), bf16[64,56,288]{2,1,0:T(8,128)(2,1)S(1)}, u32[]{:S(2)}, u32[]{:S(2)}) async-start(bf16[64,56,288]{2,1,0:T(8,128)(2,1)} %bitcast.23), calls=%async_computation.1 | async-start | bytes 5505024 | tf_op jit(solution)/shard_map/all_to_all | solution.py:40
  264.7 65.0 %all-to-all-done.1 = bf16[64,56,288]{2,1,0:T(8,128)(2,1)S(1)} async-done(((bf16[64,56,288]{2,1,0:T(8,128)(2,1)}), bf16[64,56,288]{2,1,0:T(8,128)(2,1)S(1)}, u32[]{:S(2)}, u32[]{:S(2)}) %all-to-all-start.1) | async-done | bytes 2064416 | tf_op jit(solution)/shard_map/all_to_all | solution.py:40
  329.8 2.5 gather_fusion.1
  332.3 3.7 %broadcast_select_fusion = bf16[64,56,288]{2,1,0:T(8,128)(2,1)} fusion(bf16[64,56,288]{2,1,0:T(8,128)(2,1)} %gather_fusion.1, pred[64]{0:T(512)(128)(4,1)S(1)} %compare_and_fusion), kind=kLoop, calls=%fused_computation.19 | loop fusion | flops 1032192 | bytes 4128832 | tf_op jit(solution)/shard_map/jit(_take)/select_n | solution.py:41
  (12 shorter events, 0.0 us)
Async XLA Ops:
  7.2 0.8 copy-start.1
  7.2 129.1 %all-reduce.2.cloned.1.call-start = ((), (), s32[]{:S(2)}) async-start(), calls=%async_computation.2 | async-start | bytes 5505024 | tf_op jit(solution)/shard_map/psum | solution.py:29
  241.6 3.6 %copy-start.2 = (bf16[3584,288]{0,1:T(8,128)(2,1)S(1)}, bf16[3584,288]{0,1:T(8,128)(2,1)}, u32[]{:S(2)}) copy-start(bf16[3584,288]{0,1:T(8,128)(2,1)} %fusion.4) | copy-start | bytes 6193156
  255.5 3.0 copy-start
  258.4 71.3 %all-to-all-start.1 = ((bf16[64,56,288]{2,1,0:T(8,128)(2,1)}), bf16[64,56,288]{2,1,0:T(8,128)(2,1)S(1)}, u32[]{:S(2)}, u32[]{:S(2)}) async-start(bf16[64,56,288]{2,1,0:T(8,128)(2,1)} %bitcast.23), calls=%async_computation.1 | async-start | bytes 5505024 | tf_op jit(solution)/shard_map/all_to_all | solution.py:40
Sparse Core Ops, SparseCore 0:
  10.4 125.8 all-reduce.1
where the time goes:
time: 343 us
  waiting for transfers between devices  192 us (56%)
  blocking collectives  81.9 us (24%)
  matrix products  19.5 us (6%)
  other arithmetic  16.1 us (5%)
  between operations  14.9 us (4%)
  local copies, waits for them, and re-layouts  12.1 us (4%)
  starting transfers between devices  6.3 us (2%)
    psum x1, waiting for transfers between devices, body(): total = lax.psum(grads[0], 'rep').astype(jnp.float32)  126 us
    all_to_all x1, blocking collectives, body(): lax.all_to_all(outgoing, ('fsdp', 'sub'), split_axis=0, concat_axis=1, ti...  81.9 us
    all_to_all x1, waiting for transfers between devices, body(): lax.all_to_all(pieces, ('fsdp', 'sub'), split_axis=0, concat_axis=0, tile...  65 us
    dot_general x3, matrix products, orthogonal(): jnp.dot(ycur, mixed, preferred_element_type=jnp.float32)  11.2 us
    dot_general x3, matrix products, orthogonal(): lax.dot_general(ycur, ycur, (((0,), (0,)), ((), ())), preferred_element_t...  8.28 us
  transfers between devices with their start and end apart: 2, of which 2 were waited for; matrix products, arithmetic and copies ran while one was open for 1% of the time, Pallas kernels for 0%

commit v1 on v0

v1 whole, which is shorter than its diff:
```python
import functools

import jax
import jax.numpy as jnp
from jax import lax
from jax.experimental import pallas as pl
from jax.experimental.pallas import tpu as pltpu
from jax.sharding import PartitionSpec as P

ITERS = 3
GROUP = ("fsdp", "sub")
F32 = jnp.float32
BF16 = jnp.bfloat16
SLOTS_PER_STEP = 16
VMEM_LIMIT = 56 * 1024 * 1024
SMEM = pl.BlockSpec(memory_space=pltpu.SMEM)
VMEM = pl.BlockSpec(memory_space=pltpu.VMEM)


def call(kernel, out_shape, n_in, scalars=0, scratch=(), flops=0, moved=4 << 20):
    several = isinstance(out_shape, (list, tuple))
    return pl.pallas_call(
        kernel,
        out_shape=out_shape,
        in_specs=[SMEM] * scalars + [VMEM] * n_in,
        out_specs=[VMEM] * len(out_shape) if several else VMEM,
        scratch_shapes=list(scratch),
        compiler_params=pltpu.CompilerParams(vmem_limit_bytes=VMEM_LIMIT),
        cost_estimate=pl.CostEstimate(flops=flops, bytes_accessed=moved, transcendentals=0),
    )


def shape(dims, dtype=BF16):
    return jax.ShapeDtypeStruct(dims, dtype)


def each(count, one, together=8):
    together = min(together, count)

    def several(k, carry):
        for i in range(together):
            one(k * together + i)
        return carry

    lax.fori_loop(0, count // together, several, 0)


def select_rows(first, count, width):
    row = lax.broadcasted_iota(jnp.int32, (count, width), 0)
    col = lax.broadcasted_iota(jnp.int32, (count, width), 1)
    return (col == row + first).astype(BF16)


def turn_kernel(owner_ref, first_ref, x_ref, out_ref, by_slot):
    count, rows, cols = x_ref.shape

    def place(j):
        by_slot[owner_ref[j]] = x_ref[j].astype(F32)

    each(count, place)
    pick = select_rows(first_ref[0], out_ref.shape[0], cols)
    step = SLOTS_PER_STEP
    for k in range(count // step):
        part = by_slot[k * step : (k + 1) * step].reshape(step * rows, cols).astype(BF16)
        turned = lax.dot_general(pick, part, (((1,), (1,)), ((), ())), preferred_element_type=F32)
        out_ref[:, k * step * rows : (k + 1) * step * rows] = turned.astype(BF16)


def turn(owner, first, x, picked):
    count, rows, cols = x.shape
    return call(
        turn_kernel,
        shape((picked, count * rows)),
        1,
        scalars=2,
        scratch=[pltpu.VMEM(x.shape, F32)],
        flops=2 * count * rows * cols * picked,
    )(owner, first, x)


def moment_kernel(count, total_ref, momentum_ref, new_ref, out_ref):
    total = total_ref[...].astype(F32)
    moment = 0.95 * momentum_ref[...].astype(F32) + total
    new_ref[...] = moment.astype(BF16)
    ahead = total + 0.95 * moment
    rows = total.shape[1] // count
    for s in range(count):
        block = ahead[:, s * rows : (s + 1) * rows].astype(BF16)
        out_ref[s, :, :rows] = block[:16]
        out_ref[s, :8, 64 : 64 + rows] = block[16:]


def join_kernel(x_ref, left_ref, right_ref, whole):
    count = x_ref.shape[0]
    half = left_ref.shape[1]
    rows = 2 * half // count
    for s in range(count):
        block = x_ref[s].astype(F32)
        whole[:16, s * rows : (s + 1) * rows] = block[:, :rows]
        whole[16:, s * rows : (s + 1) * rows] = block[:8, 64 : 64 + rows]
    left_ref[...] = whole[:, :half].astype(BF16)
    right_ref[...] = whole[:, half:].astype(BF16)


def untransposed(part):
    eye = select_rows(0, part.shape[0], part.shape[0])
    return lax.dot_general(part, eye, (((0,), (0,)), ((), ())), preferred_element_type=F32)


def orthogonal_kernel(count, factor, left_ref, right_ref, owned_ref, packed_ref, y_ref):
    cols, half = left_ref.shape
    squares = jnp.zeros((1, 1), F32)
    for ref in (left_ref, right_ref):
        value = ref[...].astype(F32)
        squares += jnp.sum(value * value, keepdims=True)
    scale = jnp.sqrt(squares) + 1e-07
    for k, ref in enumerate((left_ref, right_ref)):
        y_ref[:, k * half : (k + 1) * half] = (ref[...].astype(F32) / scale).astype(BF16)
    length = 2 * half
    rows = length // count
    step = SLOTS_PER_STEP
    for it in range(ITERS):
        y = y_ref[...]
        gram = lax.dot_general(y, y, (((1,), (1,)), ((), ())), preferred_element_type=F32).astype(BF16)
        square = jnp.dot(gram, gram, preferred_element_type=F32)
        mixed = (-4.775 * gram.astype(F32) + 2.0315 * square).astype(BF16)
        for k in range(count // step):
            at = slice(k * step * rows, (k + 1) * step * rows)
            old = y_ref[:, at]
            new = (3.4445 * old.astype(F32) + jnp.dot(mixed, old, preferred_element_type=F32)).astype(BF16)
            if it < ITERS - 1:
                y_ref[:, at] = new
            else:
                new = (factor * new.astype(F32)).astype(BF16)
                owned_ref[:, at] = new
                update = untransposed(new).reshape(step, rows, cols)
                main = update[:, :, :256]
                tail = jnp.concatenate(
                    [update[:, 8 * j : 8 * j + 8, 256:] for j in range(rows // 8)]
                    + [jnp.zeros((step, 8, 32), F32)],
                    axis=2,
                )
                packed_ref[k * step : (k + 1) * step] = jnp.concatenate([main, tail], axis=1).astype(BF16)


def unpack_kernel(owner_ref, packed_ref, out_ref):
    count, rows, cols = out_ref.shape

    def one(j):
        block = packed_ref[owner_ref[j]].astype(F32)
        tail = jnp.concatenate([block[rows:, 32 * k : 32 * k + 32] for k in range(rows // 8)], axis=0)
        out_ref[j] = jnp.concatenate([block[:rows], tail], axis=1).astype(BF16)

    each(count, one)


def unturn_kernel(owner_ref, x_ref, out_ref, by_slot):
    count, rows, cols = out_ref.shape
    step = SLOTS_PER_STEP
    for k in range(count // step):
        part = untransposed(x_ref[:, k * step * rows : (k + 1) * step * rows])
        by_slot[k * step : (k + 1) * step] = part.reshape(step, rows, cols)

    def one(j):
        out_ref[j] = by_slot[owner_ref[j]].astype(BF16)

    each(count, one)


def body(grads, momentum, owner):
    _, count, rows, cols = grads.shape
    reps = lax.axis_size("rep")
    share = cols // reps
    length = count * rows
    half = length // 2
    zero = jnp.zeros((1,), jnp.int32)
    first = (lax.axis_index("rep") * share).astype(jnp.int32).reshape(1)
    turned = turn(owner, zero, grads[0], cols)
    total = lax.psum_scatter(turned, "rep", scatter_dimension=0, tiled=True)
    mine = turn(owner, first, momentum, share)
    new_share, outgoing = call(
        functools.partial(moment_kernel, count), [shape((share, length)), shape((count, 16, 128))], 2
    )(total, mine)
    new_turned = lax.all_gather(new_share, "rep", axis=0, tiled=True)
    arrived = lax.all_to_all(outgoing, GROUP, split_axis=0, concat_axis=0, tiled=True)
    left, right = call(
        join_kernel, [shape((share, half))] * 2, 1, scratch=[pltpu.VMEM((share, length), F32)]
    )(arrived)
    left = lax.all_gather(left, "rep", axis=0, tiled=True)
    right = lax.all_gather(right, "rep", axis=0, tiled=True)
    factor = 0.2 * max(length, cols) ** 0.5
    owned, packed = call(
        functools.partial(orthogonal_kernel, count, factor),
        [shape((cols, length)), shape((count, rows + 8, 256))],
        2,
        scratch=[pltpu.VMEM((cols, length), BF16)],
        flops=4 * ITERS * length * cols * cols,
    )(left, right)
    packed, new_turned = lax.optimization_barrier((packed, new_turned))
    returned = lax.all_to_all(packed, GROUP, split_axis=0, concat_axis=0, tiled=True)
    new_momentum = call(
        unturn_kernel,
        shape((count, rows, cols)),
        1,
        scalars=1,
        scratch=[pltpu.VMEM((count, rows, cols), F32)],
        flops=2 * length * cols * cols,
    )(owner, new_turned)
    update = call(unpack_kernel, shape((count, rows, cols)), 1, scalars=1)(owner, returned)
    return (new_momentum, update, owned.T[None])


def solution(mesh):
    placed = (P("rep", None, GROUP, None), P(None, GROUP, None), P())
    return jax.shard_map(
        body,
        mesh=mesh,
        in_specs=placed,
        out_specs=(P(None, GROUP, None), P(None, GROUP, None), P(GROUP, None, None)),
        check_vma=False,
    )
```

time: 343 us -> 261 us (0.76)
  waiting for transfers between devices: 192 us -> 104 us
  Pallas kernels: 0 us -> 35.2 us
  matrix products: 19.5 us -> 0 us
  other arithmetic: 16.1 us -> 0 us
  starting transfers between devices: 6.3 us -> 17.9 us
  local copies, waits for them, and re-layouts: 12.1 us -> 1.34 us
  blocking collectives: 81.9 us -> 87.7 us
    psum x1 -> x0, waiting for transfers between devices: 126 us -> none  [body(): total = lax.psum(grads[0], 'rep').astype(jnp.float32)]
    all_gather x0 -> x2, blocking collectives: none -> 58.5 us  [the longest x1 33.8 us: body(): left = lax.all_gather(left, 'rep', axis=0, tiled=True)]
    reduce_scatter x0 -> x1, waiting for transfers between devices: none -> 58.2 us  [body(): total = lax.psum_scatter(turned, 'rep', scatter_dimension=0, tiled=True)]
    all_to_all x1, blocking collectives: 81.9 us -> 29.2 us  [body(): lax.all_to_all(outgoing, GROUP, split_axis=0, concat_axis=0, tiled=True)]
    pallas_call x0 -> x7, Pallas kernels: none -> 35.2 us  [the longest x1 13.6 us: body(): call(functools.partial(orthogonal_kernel, count, factor), [shape((cols, l...]
    dot_general x6 -> x0, matrix products: 19.5 us -> none  [the longest x3 11.2 us: orthogonal(): jnp.dot(ycur, mixed, preferred_element_type=jnp.float32)]
    all_to_all x1, waiting for transfers between devices: 65 us -> 46.1 us  [body(): lax.all_to_all(packed, GROUP, split_axis=0, concat_axis=0, tiled=True)]
    all_to_all x1, starting transfers between devices: 6.26 us -> 17.8 us  [body(): lax.all_to_all(packed, GROUP, split_axis=0, concat_axis=0, tiled=True)]
  transfers between devices with their start and end apart: 2 -> 3, of which waited for: 2 -> 2; matrix products, arithmetic and copies ran while one was open for 1% -> 0% of each run, Pallas kernels for 0% -> 9%
where the time goes in v1:
time: 261 us
  waiting for transfers between devices  104 us (40%)
  blocking collectives  87.7 us (34%)
  Pallas kernels  35.2 us (13%)
  starting transfers between devices  17.9 us (7%)
  between operations  14.1 us (5%)
    reduce_scatter x1, waiting for transfers between devices, body(): total = lax.psum_scatter(turned, 'rep', scatter_dimension=0, tiled=True)  58.2 us
    all_to_all x1, waiting for transfers between devices, body(): lax.all_to_all(packed, GROUP, split_axis=0, concat_axis=0, tiled=True)  46.1 us
    all_gather x1, blocking collectives, body(): left = lax.all_gather(left, 'rep', axis=0, tiled=True)  33.8 us
    all_to_all x1, blocking collectives, body(): lax.all_to_all(outgoing, GROUP, split_axis=0, concat_axis=0, tiled=True)  29.2 us
    all_gather x1, blocking collectives, body(): right = lax.all_gather(right, 'rep', axis=0, tiled=True)  24.8 us
    all_to_all x1, starting transfers between devices, body(): lax.all_to_all(packed, GROUP, split_axis=0, concat_axis=0, tiled=True)  17.8 us
    pallas_call x1, Pallas kernels, body(): call(functools.partial(orthogonal_kernel, count, factor), [shape((cols, l...  13.6 us
    pallas_call x2, Pallas kernels, turn(): call(turn_kernel, shape((picked, count * rows)), 1, scalars=2, scratch=[p...  8.75 us
  transfers between devices with their start and end apart: 3, of which 2 were waited for; matrix products, arithmetic and copies ran while one was open for 0% of the time, Pallas kernels for 9%

profile of v1, /device:TPU:1, one launch (start us, length us, event | category | flops | bytes accessed | tf_op | source)
XLA Modules:
  0.0 260.6 jit_solution(13085979427607471674)
XLA Ops:
  7.2 0.0 reduce-scatter.2.cloned.1.call-start
  7.2 4.9 %shard_map.58 = bf16[288,3584]{1,0:T(8,128)(2,1)} custom-call(s32[64]{0:T(128)} %owner_ref.7, s32[1]{0:T(128)} %constant.1.clone.1.first_ref, bf16[64,56,288]{2,1,0:T(8,128)(2,1)} %bitcast.5), custom_call_target="tpu_custom_call" | custom-call | flops 594542592 | bytes 4194304 | tf_op jit(solution)/shard_map/pallas_call | solution.py:71
  12.1 0.0 reduce-scatter.2.cloned.1.call-update
  12.2 0.0 all-gather.2.cloned.1.call-start
  12.2 3.8 %shard_map.59.momentum_ref = bf16[24,3584]{1,0:T(8,128)(2,1)} custom-call(s32[64]{0:T(128)} %owner_ref.7, s32[1]{0:T(128)} %bitcast.1.first_ref, bf16[64,56,288]{2,1,0:T(8,128)(2,1)} %x_ref.1), custom_call_target="tpu_custom_call" | custom-call | flops 49545216 | bytes 4194304 | tf_op jit(solution)/shard_map/pallas_call | solution.py:71
  16.0 58.2 %reduce-scatter.2.cloned.1.call-done.total_ref = bf16[24,3584]{1,0:T(8,128)(2,1)} async-done(((bf16[288,3584]{1,0:T(8,128)(2,1)}), bf16[24,3584]{1,0:T(8,128)(2,1)}) %reduce-scatter.2.cloned.1.call-update) | async-done | bytes 172048 | tf_op jit(solution)/shard_map/reduce_scatter | solution.py:179
  74.3 2.0 shard_map.60
  76.3 0.0 all-gather.2.cloned.1.call-update
  76.3 29.2 %all_to_all.10.x_ref = bf16[64,16,128]{2,1,0:T(8,128)(2,1)} all-to-all(bf16[64,16,128]{2,1,0:T(8,128)(2,1)} %get-tuple-element.11), channel_id=1, replica_groups=mesh['rep'=12,'fsdp'=32,'sub'=2] {'fsdp','sub'}, dimensions={0} | all-to-all | bytes 524288 | tf_op jit(solution)/shard_map/all_to_all | solution.py:185
  105.5 1.8 shard_map.61
  107.3 33.8 %all_gather.9.left_ref = bf16[288,1792]{1,0:T(8,128)(2,1)} all-gather(bf16[24,1792]{1,0:T(8,128)(2,1)} %get-tuple-element.12), channel_id=1, replica_groups=mesh['rep'=12,'fsdp'=32,'sub'=2] {'rep'}, dimensions={0}, use_global_device_ids=true | all-gather | bytes 1118208 | tf_op jit(solution)/shard_map/all_gather | solution.py:189
  141.1 24.8 %all_gather.10.right_ref = bf16[288,1792]{1,0:T(8,128)(2,1)} all-gather(bf16[24,1792]{1,0:T(8,128)(2,1)} %get-tuple-element.13), channel_id=1, replica_groups=mesh['rep'=12,'fsdp'=32,'sub'=2] {'rep'}, dimensions={0}, use_global_device_ids=true | all-gather | bytes 1118208 | tf_op jit(solution)/shard_map/all_gather | solution.py:190
  165.8 13.6 %shard_map.62 = (bf16[288,3584]{1,0:T(8,128)(2,1)}, bf16[64,64,256]{2,1,0:T(8,128)(2,1)}) custom-call(bf16[288,1792]{1,0:T(8,128)(2,1)} %all_gather.9.left_ref, bf16[288,1792]{1,0:T(8,128)(2,1)} %all_gather.10.right_ref), custom_call_target="tpu_custom_call" | custom-call | flops 3567255552 | bytes 4194304 | tf_op jit(solution)/shard_map/pallas_call | solution.py:192
  179.4 0.0 all-gather.2.cloned.1.call-done.x_ref
  179.4 17.8 %all-to-all-start.1 = ((bf16[64,64,256]{2,1,0:T(8,128)(2,1)}), bf16[64,64,256]{2,1,0:T(8,128)(2,1)S(1)}, u32[]{:S(2)}, u32[]{:S(2)}) async-start(bf16[64,64,256]{2,1,0:T(8,128)(2,1)} %get-tuple-element.17), calls=%async_computation.2 | async-start | bytes 4194304 | tf_op jit(solution)/shard_map/all_to_all | solution.py:200
  197.2 5.1 %shard_map.63 = bf16[64,56,288]{2,1,0:T(8,128)(2,1)} custom-call(s32[64]{0:T(128)} %owner_ref.7, bf16[288,3584]{1,0:T(8,128)(2,1)} %all-gather.2.cloned.1.call-done.x_ref), custom_call_target="tpu_custom_call" | custom-call | flops 594542592 | bytes 4194304 | tf_op jit(solution)/shard_map/pallas_call | solution.py:201
  202.3 46.1 %all-to-all-done.1.packed_ref = bf16[64,64,256]{2,1,0:T(8,128)(2,1)S(1)} async-done(((bf16[64,64,256]{2,1,0:T(8,128)(2,1)}), bf16[64,64,256]{2,1,0:T(8,128)(2,1)S(1)}, u32[]{:S(2)}, u32[]{:S(2)}) %all-to-all-start.1) | async-done | bytes 2097184 | tf_op jit(solution)/shard_map/all_to_all | solution.py:200
  248.5 0.0 copy-start
  248.5 1.3 copy-done
  249.8 3.9 %shard_map.64 = bf16[64,56,288]{2,1,0:T(8,128)(2,1)} custom-call(s32[64]{0:T(128)} %owner_ref.7, bf16[64,64,256]{2,1,0:T(8,128)(2,1)} %copy-done), custom_call_target="tpu_custom_call" | custom-call | bytes 4194304 | tf_op jit(solution)/shard_map/pallas_call | solution.py:209
Async XLA Ops:
  7.2 67.1 %reduce-scatter.2.cloned.1.call-start = ((), (), s32[]{:S(2)}) async-start(), calls=%async_computation.3 | async-start | bytes 2236416 | tf_op jit(solution)/shard_map/reduce_scatter | solution.py:179
  12.2 167.3 %all-gather.2.cloned.1.call-start = ((), (), s32[]{:S(2)}) async-start(), calls=%async_computation.4 | async-start | bytes 2236416 | tf_op jit(solution)/shard_map/all_gather | solution.py:184
  179.4 69.0 %all-to-all-start.1 = ((bf16[64,64,256]{2,1,0:T(8,128)(2,1)}), bf16[64,64,256]{2,1,0:T(8,128)(2,1)S(1)}, u32[]{:S(2)}, u32[]{:S(2)}) async-start(bf16[64,64,256]{2,1,0:T(8,128)(2,1)} %get-tuple-element.17), calls=%async_computation.2 | async-start | bytes 4194304 | tf_op jit(solution)/shard_map/all_to_all | solution.py:200
  248.5 1.3 copy-start
Sparse Core Ops, SparseCore 0:
  12.3 61.9 reduce-scatter.1
  77.5 62.9 all-gather.1
